TPU v7x, 32 devices: a whole 2x2x4 slice. The times are simulated.
32 devices in a mesh: row: 8 (over z, y), col: 4 (over x, core).
Axes of the slice: x: 2, y: 2, z: 4, core: 2. Of those that a mesh axis runs over, the one named last changes fastest.
Arguments:
- counts: int32 [1024, 262144], P('row', 'col'), may hold values from 0 to 7, as said below
- row_total: float32 [1024], P('row'), may hold values from 1 to 3670016, as said below
- col_total: float32 [262144], P('col'), may hold values from 1 to 3670528, as said below
- grand_total: float32 [1], replicated, as said below
- sketch: float32 [262144, 96], P(('col', 'row')), may hold values from -0.00036621094 to 0.00036621094
Outputs:
- column_factors: float32 [262144, 96], P(('col', 'row'))
- gram_factor: float32 [96, 96], replicated
Inputs may be any that keep to these rules, and one draw needn't show every extreme that they name: About half of the counts are zero. `row_total`: each row's total is its counts' sum times a factor between 1 and 2. `col_total`: each item's total is its counts' sum over the slab plus one, times 262144 / 1024, times a factor between 1 and 2. `grand_total`: the grand total is the sum of col_total times a factor between 1 and 1.25.
All inputs are finite; a program needn't handle non-finite values.
Results may differ from a plain program's by a relative error of at most 0.0003.
Values sent between devices are 32-bit elements; how exact they have to be, the bound alone decides.
A program may use at most 128 MiB of HBM per device.

v0:
```python
import jax
import jax.numpy as jnp
from jax import lax
from jax.sharding import PartitionSpec as P


def per_device(counts, row_total, col_total, grand_total, sketch):
    row_log = jnp.log(grand_total[0]) - jnp.log(row_total)
    counts_float = counts.astype(jnp.float32)
    pmi = jnp.log(jnp.maximum(counts_float, 1.0)) + row_log[:, None] - jnp.log(col_total)[None, :]
    ppmi_tile = jnp.where(counts > 0, jnp.maximum(pmi, 0.0), 0.0)
    columns = ppmi_tile
    partial_image = jnp.dot(
        columns,
        lax.all_gather(sketch, "row", axis=0, tiled=True),
        precision=lax.Precision.HIGHEST,
        preferred_element_type=jnp.float32,
    )
    image = lax.psum(partial_image, "col")
    gram_local = jnp.dot(
        image.T, image, precision=lax.Precision.HIGHEST, preferred_element_type=jnp.float32
    )
    gram_matrix = lax.psum(gram_local, "row")
    factor = jnp.linalg.cholesky(gram_matrix)
    columns = ppmi_tile
    summed_columns = lax.psum_scatter(
        lax.dot_general(
            columns,
            image,
            (((0,), (0,)), ((), ())),
            precision=lax.Precision.HIGHEST,
            preferred_element_type=jnp.float32,
        ),
        "row",
        scatter_dimension=0,
        tiled=True,
    )
    column_factors = jax.scipy.linalg.solve_triangular(factor, summed_columns.T, lower=True).T
    return (column_factors, factor)


def solution(mesh):
    return jax.shard_map(
        per_device,
        mesh=mesh,
        in_specs=(P("row", "col"), P("row"), P("col"), P(), P(("col", "row"), None)),
        out_specs=(P(("col", "row"), None), P()),
        check_vma=False,
    )
```

profile of v0, /device:TPU:0, one launch (start us, length us, event | category | flops | bytes accessed | tf_op | source)
XLA Modules:
  0.0 1010.4 jit_solution(6782298470812548556)
XLA Ops:
  7.2 0.0 all-gather.2.cloned.1.call-start
  7.2 0.7 all-gather.2.cloned.1.call-update
  7.9 0.0 reduce-scatter.2.cloned.1.call-start
  7.9 1.0 log.19
  9.6 0.7 log_subtract_fusion
  10.3 482.4 %all-gather.2.cloned.1.call-done = f32[65536,96]{0,1:T(8,128)} async-done(((f32[8192,96]{0,1:T(8,128)}), f32[65536,96]{0,1:T(8,128)}) %all-gather.2.cloned.1.call-update) | async-done | bytes 25165840 | tf_op jit(solution)/shard_map/all_gather | solution.py:15
  492.7 46.9 %fusion.1 = f32[128,96]{0,1:T(8,128)S(1)} fusion(f32[65536,96]{0,1:T(8,128)} %all-gather.2.cloned.1.call-done, s32[128,65536]{1,0:T(8,128)} %param.5, f32[65536]{0:T(1024)S(1)} %log.19, f32[128]{0:T(128)S(1)} %log_subtract_fusion), kind=kOutput, calls=%fused_computation.2 | convolution fusion | flops 9722396672 | bytes 59032064 | tf_op jit(solution)/shard_map/dot_general | solution.py:13
  539.6 11.7 %psum.14 = f32[128,96]{0,1:T(8,128)S(1)} all-reduce(f32[128,96]{0,1:T(8,128)S(1)} %fusion.1), channel_id=1, replica_groups=mesh['row'=8,'col'=4] {'col'}, use_global_device_ids=true, to_apply=%region_0.1 | all-reduce | flops 12288 | bytes 98304 | tf_op jit(solution)/shard_map/psum | solution.py:19
  551.4 41.5 %fusion = f32[65536,96]{0,1:T(8,128)} fusion(f32[128,96]{0,1:T(8,128)S(1)} %psum.14, s32[128,65536]{1,0:T(8,128)} %param.5, f32[65536]{0:T(1024)S(1)} %log.19, f32[128]{0:T(128)S(1)} %log_subtract_fusion), kind=kOutput, calls=%fused_computation.1 | convolution fusion | flops 9722396672 | bytes 59032064 | tf_op jit(solution)/shard_map/dot_general | solution.py:27
  592.9 0.0 reduce-scatter.2.cloned.1.call-update
  592.9 0.2 fusion.21
  593.1 38.4 %psum.15 = f32[96,96]{0,1:T(8,128)S(1)} all-reduce(f32[96,96]{0,1:T(8,128)S(1)} %fusion.21), channel_id=1, replica_groups=mesh['row'=8,'col'=4] {'row'}, use_global_device_ids=true, to_apply=%region_2.3 | all-reduce | flops 9216 | bytes 73728 | tf_op jit(solution)/shard_map/psum | solution.py:23
  631.6 0.1 copy.10
  631.7 8.8 cholesky.16
  640.5 0.6 compare_reduce_fusion
  641.1 1.3 select_bitcast_fusion
  642.4 7.4 custom-call.7
  649.8 347.3 %reduce-scatter.2.cloned.1.call-done = f32[8192,96]{0,1:T(8,128)} async-done(((f32[65536,96]{0,1:T(8,128)}), f32[8192,96]{0,1:T(8,128)}) %reduce-scatter.2.cloned.1.call-update) | async-done | bytes 3145744 | tf_op jit(solution)/shard_map/reduce_scatter | solution.py:26
  997.1 6.5 fusion.12
  (2 shorter events, 0.0 us)
Async XLA Ops:
  7.2 485.5 %all-gather.2.cloned.1.call-start = ((), (), s32[]{:S(2)}) async-start(), calls=%async_computation.1 | async-start | bytes 28311552 | tf_op jit(solution)/shard_map/all_gather | solution.py:15
  7.9 989.2 %reduce-scatter.2.cloned.1.call-start = ((), (), s32[]{:S(2)}) async-start(), calls=%async_computation.2 | async-start | bytes 28311552 | tf_op jit(solution)/shard_map/reduce_scatter | solution.py:26
Sparse Core Ops, SparseCore 0:
  9.5 483.1 all-gather.1
  593.0 404.0 reduce-scatter.1
where the time goes:
time: 1010 us
  waiting for transfers between devices  830 us (82%)
  matrix products  95.1 us (9%)
  blocking collectives  50.2 us (5%)
  other arithmetic  18.8 us (2%)
  between operations  14.8 us (1%)
    all_gather x1, waiting for transfers between devices, per_device(): lax.all_gather(sketch, 'row', axis=0, tiled=True)  482 us
    reduce_scatter x1, waiting for transfers between devices, per_device(): lax.psum_scatter(lax.dot_general(columns, image, (((0,), (0,)), ((), ()))...  347 us
    dot_general x1, matrix products, per_device(): jnp.dot(columns, lax.all_gather(sketch, 'row', axis=0, tiled=True), preci...  46.9 us
    dot_general x1, matrix products, per_device(): lax.dot_general(columns, image, (((0,), (0,)), ((), ())), precision=lax.P...  41.5 us
    psum x1, blocking collectives, per_device(): gram_matrix = lax.psum(gram_local, 'row')  38.4 us
  transfers between devices with their start and end apart: 2, of which 2 were waited for; matrix products, arithmetic and copies ran while one was open for 2% of the time, Pallas kernels for 0%

commit v1 on v0

v1 whole, which is shorter than its diff:
```python
import functools

import jax
import jax.numpy as jnp
from jax import lax
from jax.experimental import pallas as pl
from jax.experimental.pallas import tpu as pltpu
from jax.sharding import PartitionSpec as P

MESH = pl.DeviceIdType.MESH
VMEM_BYTES = 56 * 2**20
F32, BF16 = jnp.float32, jnp.bfloat16


def ring_place(row, n):
    odd = lax.rem(row, 2)
    up = lax.div(row, 2)
    return (1 - odd) * up + odd * (n - 1 - up)


def ring_row(place, n):
    back = lax.div(place, n // 2)
    return (1 - back) * 2 * place + back * (2 * (n - 1 - place) + 1)


def neighbours(n):
    me = ring_place(lax.axis_index("row"), n)
    after = ring_row(lax.rem(me + 1, n), n)
    before = ring_row(lax.rem(me + n - 1, n), n)
    return me, after, before


def meet(after, before):
    barrier = pltpu.get_barrier_semaphore()
    for row in (after, before):
        pl.semaphore_signal(
            barrier, inc=1, device_id=(row, lax.axis_index("col")), device_id_type=MESH
        )
    pl.semaphore_wait(barrier, 2)


def split(x):
    high = x.astype(BF16)
    return high, (x - high.astype(F32)).astype(BF16)


def ppmi_parts(counts, row_log, col_total):
    pmi = jnp.log(jnp.maximum(counts.astype(F32), 1.0)) + row_log - jnp.log(col_total)
    ppmi = jnp.where(counts > 0, jnp.maximum(pmi, 0.0), 0.0)
    return jnp.concatenate(split(ppmi), axis=0)


def tile_width(half):
    width = 1024
    while half % width:
        width //= 2
    return width


def columns_of(place, half, width, n):
    return pl.multiple_of(ring_row(place, n) * (2 * width) + half * width, 128)


def counts_copy(counts_ref, held, sem, item, start, width):
    slot = lax.rem(item, 2)
    return pltpu.make_async_copy(
        counts_ref.at[:, pl.ds(start, width)], held.at[slot], sem.at[slot]
    )


def gather_kernel(
    n, counts_ref, row_log_ref, col_ref, sketch_ref, image_ref,
    buf, held, total, send_sem, recv_sem, counts_sem, own_sem,
):
    width = buf.shape[3]
    rank = buf.shape[2]
    rows = row_log_ref.shape[0]
    tile = tile_width(width)
    me, after, before = neighbours(n)
    col = lax.axis_index("col")

    def where_of(item):
        extra = lax.max(item - 2, 0)
        far = lax.min(lax.div(item, 2), 1)
        way = far * lax.rem(extra, 2)
        slot = (1 - far) * item + far * (2 + lax.div(extra, 2))
        distance = lax.div(slot, 2)
        odd = lax.rem(slot, 2)
        half = (1 - way) * odd + way * (1 - odd)
        place = lax.rem(me + n + (2 * way - 1) * distance, n)
        return way, slot, columns_of(place, half, width, n)

    def send(way, slot):
        return pltpu.make_async_remote_copy(
            src_ref=buf.at[way, slot],
            dst_ref=buf.at[way, slot + 2],
            send_sem=send_sem.at[way, slot],
            recv_sem=recv_sem.at[way, slot],
            device_id=((1 - way) * after + way * before, col),
            device_id_type=MESH,
        )

    def counts_of(item):
        return counts_copy(counts_ref, held, counts_sem, item, where_of(item)[2], width)

    own = [
        pltpu.make_async_copy(
            sketch_ref.at[:, pl.ds((slot if way == 0 else 1 - slot) * width, width)],
            buf.at[way, slot],
            own_sem.at[way, slot],
        )
        for slot in range(2)
        for way in range(2)
    ]
    for copy in own:
        copy.start()
    counts_of(0).start()
    meet(after, before)
    for at, copy in enumerate(own):
        copy.wait()
        send(at % 2, at // 2).start()
    total[...] = jnp.zeros_like(total)

    def step(item, carry):
        way, slot, start = where_of(item)

        @pl.when(item + 1 < 2 * n)
        def _():
            counts_of(item + 1).start()

        @pl.when(item >= 2)
        def _():
            send(way, slot - 2).wait_recv()

            @pl.when(slot <= n - 2)
            def _():
                send(way, slot).start()

        counts_of(item).wait()
        at = lax.rem(item, 2)

        def piece(t, carry):
            here = pl.ds(pl.multiple_of(t * tile, tile), tile)
            parts = ppmi_parts(
                held[at, :, here],
                row_log_ref[...],
                col_ref[:, pl.ds(pl.multiple_of(start + t * tile, 128), tile)],
            )
            high, low = split(buf[way, slot, :, here])
            gap = jnp.zeros((128 - rank % 128, tile), BF16)
            test = jnp.concatenate([high, gap, low, gap], axis=0)
            total[...] += lax.dot_general(
                parts, test, (((1,), (1,)), ((), ())), preferred_element_type=F32
            )
            return carry

        lax.fori_loop(0, width // tile, piece, 0)
        return carry

    lax.fori_loop(0, 2 * n, step, 0)
    wide = total.shape[1] // 2
    both = total[:rows, :] + total[rows:, :]
    image_ref[...] = (both[:, :wide] + both[:, wide:])[:, :rank]

    def sent(slot, carry):
        send(0, slot).wait_send()
        send(1, slot).wait_send()
        return carry

    lax.fori_loop(0, n - 1, sent, 0)


def scatter_kernel(
    n, counts_ref, row_log_ref, col_ref, image_ref, out_ref,
    buf, held, left, send_sem, recv_sem, counts_sem,
):
    width = buf.shape[3]
    rank = buf.shape[2]
    tile = tile_width(width)
    me, after, before = neighbours(n)
    col = lax.axis_index("col")

    def where_of(item):
        way = lax.rem(item, 2)
        own = lax.div(item, 2 * n - 2)
        slot = (1 - own) * (n - lax.div(item, 2)) + own * (n + 1)
        distance = (1 - own) * lax.div(slot, 2)
        odd = lax.rem(slot, 2)
        half = (1 - own) * ((1 - way) * odd + way * (1 - odd)) + own * way
        place = lax.rem(me + n + (1 - 2 * way) * distance, n)
        return way, slot, columns_of(place, half, width, n)

    def send(way, slot):
        return pltpu.make_async_remote_copy(
            src_ref=buf.at[way, slot + 2],
            dst_ref=buf.at[way, slot],
            send_sem=send_sem.at[way, slot],
            recv_sem=recv_sem.at[way, slot],
            device_id=((1 - way) * after + way * before, col),
            device_id_type=MESH,
        )

    def counts_of(item):
        return counts_copy(counts_ref, held, counts_sem, item, where_of(item)[2], width)

    counts_of(0).start()
    high, low = split(image_ref[...])
    left[...] = jnp.concatenate(
        [jnp.concatenate([high, high], axis=1), jnp.concatenate([low, low], axis=1)], axis=0
    )
    meet(after, before)

    def step(item, carry):
        way, slot, start = where_of(item)
        arrives = slot <= n - 2

        @pl.when(item + 1 < 2 * n)
        def _():
            counts_of(item + 1).start()

        counts_of(item).wait()

        @pl.when(arrives)
        def _():
            send(way, slot).wait_recv()

        at = lax.rem(item, 2)

        def piece(t, carry):
            here = pl.ds(pl.multiple_of(t * tile, tile), tile)
            parts = ppmi_parts(
                held[at, :, here],
                row_log_ref[...],
                col_ref[:, pl.ds(pl.multiple_of(start + t * tile, 128), tile)],
            )
            product = jnp.dot(left[...], parts, preferred_element_type=F32)
            product = product[:rank] + product[rank:]

            @pl.when(arrives)
            def _():
                buf[way, slot, :, here] = buf[way, slot, :, here] + product

            @pl.when(jnp.logical_not(arrives))
            def _():
                buf[way, slot, :, here] = product

            return carry

        lax.fori_loop(0, width // tile, piece, 0)

        @pl.when(slot <= n)
        def _():
            send(way, slot - 2).start()

        return carry

    lax.fori_loop(0, 2 * n, step, 0)
    for slot in (1, 0):
        for way in range(2):
            send(way, slot).wait_recv()
    for half in range(2):
        def add(t, carry, half=half):
            here = pl.ds(pl.multiple_of(t * tile, tile), tile)
            there = pl.ds(pl.multiple_of(half * width + t * tile, tile), tile)
            out_ref[:, there] = (
                buf[half, n + 1, :, here] + buf[0, half, :, here] + buf[1, 1 - half, :, here]
            )
            return carry

        lax.fori_loop(0, width // tile, add, 0)

    def sent(slot, carry):
        send(0, slot).wait_send()
        send(1, slot).wait_send()
        return carry

    lax.fori_loop(0, n - 1, sent, 0)


def per_device(n, counts, row_total, col_total, grand_total, sketch):
    rows, columns = counts.shape
    shard, rank = sketch.shape
    width = shard // 2
    row_log = (jnp.log(grand_total[0]) - jnp.log(row_total))[:, None]
    col_row = col_total[None, :]
    vmem, anywhere = pl.BlockSpec(memory_space=pltpu.VMEM), pl.BlockSpec(memory_space=pl.ANY)
    cost = pl.CostEstimate(
        flops=8 * rows * columns * rank, bytes_accessed=4 * rows * columns, transcendentals=rows * columns
    )
    dma = pltpu.SemaphoreType.DMA
    padded = (rank + 127) // 128 * 128

    partial_image = pl.pallas_call(
        functools.partial(gather_kernel, n),
        out_shape=jax.ShapeDtypeStruct((rows, rank), F32),
        in_specs=[anywhere, vmem, vmem, anywhere],
        out_specs=vmem,
        scratch_shapes=[
            pltpu.VMEM((2, n + 1, rank, width), F32),
            pltpu.VMEM((2, rows, width), jnp.int32),
            pltpu.VMEM((2 * rows, 2 * padded), F32),
            dma((2, n - 1)),
            dma((2, n - 1)),
            dma((2,)),
            dma((2, 2)),
        ],
        compiler_params=pltpu.CompilerParams(
            collective_id=0, has_side_effects=True, vmem_limit_bytes=VMEM_BYTES
        ),
        cost_estimate=cost,
        name="gather_image",
    )(counts, row_log, col_row, sketch.T)

    image = lax.psum(partial_image, "col")
    gram_local = jnp.dot(
        image.T, image, precision=lax.Precision.HIGHEST, preferred_element_type=F32
    )
    gram_matrix = lax.psum(gram_local, "row")
    factor = jnp.linalg.cholesky(gram_matrix)

    summed = pl.pallas_call(
        functools.partial(scatter_kernel, n),
        out_shape=jax.ShapeDtypeStruct((rank, shard), F32),
        in_specs=[anywhere, vmem, vmem, vmem],
        out_specs=vmem,
        scratch_shapes=[
            pltpu.VMEM((2, n + 2, rank, width), F32),
            pltpu.VMEM((2, rows, width), jnp.int32),
            pltpu.VMEM((2 * rank, 2 * rows), BF16),
            dma((2, n - 1)),
            dma((2, n - 1)),
            dma((2,)),
        ],
        compiler_params=pltpu.CompilerParams(
            collective_id=1, has_side_effects=True, vmem_limit_bytes=VMEM_BYTES
        ),
        cost_estimate=cost,
        name="scatter_columns",
    )(counts, row_log, col_row, image.T)
    column_factors = jax.scipy.linalg.solve_triangular(factor, summed, lower=True).T
    return (column_factors, factor)


def solution(mesh):
    return jax.shard_map(
        functools.partial(per_device, mesh.shape["row"]),
        mesh=mesh,
        in_specs=(P("row", "col"), P("row"), P("col"), P(), P(("col", "row"), None)),
        out_specs=(P(("col", "row"), None), P()),
        check_vma=False,
    )
```

time: 1010 us -> 562 us (0.56)
  waiting for transfers between devices: 830 us -> 0 us
  Pallas kernels: 0 us -> 485 us
  matrix products: 95.1 us -> 6.73 us
  between operations: 14.8 us -> 1.41 us
    pallas_call x0 -> x2, Pallas kernels: none -> 485 us  [the longest x1 246 us: per_device(): pl.pallas_call(functools.partial(gather_kernel, n), out_shape=jax.ShapeDt...]
    all_gather x1 -> x0, waiting for transfers between devices: 482 us -> none  [per_device(): lax.all_gather(sketch, 'row', axis=0, tiled=True)]
    reduce_scatter x1 -> x0, waiting for transfers between devices: 347 us -> none  [per_device(): lax.psum_scatter(lax.dot_general(columns, image, (((0,), (0,)), ((), ()))...]
    dot_general x2 -> x0, matrix products: 88.4 us -> none  [the longest x1 46.9 us: per_device(): jnp.dot(columns, lax.all_gather(sketch, 'row', axis=0, tiled=True), preci...]
  transfers between devices with their start and end apart: 2 -> 0, of which waited for: 2 -> 0; matrix products, arithmetic and copies ran while one was open for 2% -> 0% of each run, Pallas kernels for 0% -> 0%
where the time goes in v1:
time: 562 us
  Pallas kernels  485 us (86%)
  blocking collectives  47.6 us (8%)
  other arithmetic  18.9 us (3%)
  matrix products  6.73 us (1%)
    pallas_call x1, Pallas kernels, per_device(): pl.pallas_call(functools.partial(gather_kernel, n), out_shape=jax.ShapeDt...  246 us
    pallas_call x1, Pallas kernels, per_device(): pl.pallas_call(functools.partial(scatter_kernel, n), out_shape=jax.ShapeD...  239 us
    psum x1, blocking collectives, per_device(): gram_matrix = lax.psum(gram_local, 'row')  36.9 us

profile of v1, /device:TPU:0, one launch (start us, length us, event | category | flops | bytes accessed | tf_op | source)
XLA Modules:
  0.0 561.5 jit_solution(3514690124144934984)
XLA Ops:
  1.3 0.7 subtract_bitcast_fusion
  2.0 0.7 copy.9.row_log_ref
  2.7 246.4 %gather_image.1 = f32[128,96]{1,0:T(8,128)} custom-call(s32[128,65536]{1,0:T(8,128)} %counts_ref.3, f32[128,1]{1,0:T(8,128)} %copy.9.row_log_ref, f32[1,65536]{1,0:T(1,128)} %bitcast.19, f32[96,8192]{1,0:T(8,128)} %bitcast.18), custom_call_target="tpu_custom_call" | custom-call | flops 6442450944 | bytes 33554432 | tf_op jit(solution)/shard_map/gather_image/pallas_call | solution.py:293
  249.2 0.9 copy.8
  250.1 10.6 %psum.14 = f32[128,96]{0,1:T(8,128)S(1)} all-reduce(f32[128,96]{0,1:T(8,128)S(1)} %copy.8), channel_id=1, replica_groups=mesh['row'=8,'col'=4] {'col'}, use_global_device_ids=true, to_apply=%region_0.0 | all-reduce | flops 12288 | bytes 98304 | tf_op jit(solution)/shard_map/psum | solution.py:314
  260.7 0.0 copy-start
  260.7 0.2 fusion.3
  261.0 36.9 %psum.15 = f32[96,96]{0,1:T(8,128)S(1)} all-reduce(f32[96,96]{0,1:T(8,128)S(1)} %fusion.3), channel_id=1, replica_groups=mesh['row'=8,'col'=4] {'row'}, use_global_device_ids=true, to_apply=%region_1.0 | all-reduce | flops 9216 | bytes 73728 | tf_op jit(solution)/shard_map/psum | solution.py:318
  297.9 0.1 copy.11
  298.0 8.8 %cholesky.16 = f32[96,96]{1,0:T(8,128)S(1)} custom-call(f32[96,96]{1,0:T(8,128)S(1)} %fusion.2), custom_call_target="Cholesky" | custom-call | tf_op jit(solution)/shard_map/jit(cholesky)/cholesky | solution.py:319
  306.8 0.7 compare_reduce_fusion
  307.5 1.3 select_bitcast_fusion
  308.9 7.4 %custom-call.7 = f32[1,96,96]{1,2,0:T(8,128)S(1)} custom-call(f32[1,96,96]{2,1,0:T(8,128)S(1)} %get-tuple-element.2), custom_call_target="InvertDiagBlocksLowerTriangular" | custom-call | tf_op jit(solution)/shard_map/jit(_solve_triangular)/triangular_solve | solution.py:340
  316.2 0.0 copy-done
  316.2 238.8 %scatter_columns.1 = f32[96,8192]{1,0:T(8,128)} custom-call(s32[128,65536]{1,0:T(8,128)} %counts_ref.3, f32[128,1]{1,0:T(8,128)} %copy.9.row_log_ref, f32[1,65536]{1,0:T(1,128)} %bitcast.20, f32[96,128]{1,0:T(8,128)} %bitcast.21), custom_call_target="tpu_custom_call" | custom-call | flops 6442450944 | bytes 33554432 | tf_op jit(solution)/shard_map/scatter_columns/pallas_call | solution.py:321
  555.0 6.5 %fusion = f32[8192,96]{0,1:T(8,128)} fusion(f32[96,8192]{1,0:T(8,128)} %scatter_columns.1, f32[1,96,96]{1,2,0:T(8,128)S(1)} %custom-call.7), kind=kOutput, calls=%fused_computation | convolution fusion | flops 905969664 | bytes 6328320 | tf_op jit(solution)/shard_map/jit(_solve_triangular)/triangular_solve | solution.py:340
  (2 shorter events, 0.0 us)
Async XLA Ops:
  260.7 55.5 %copy-start = (f32[128,96]{0,1:T(8,128)}, f32[128,96]{0,1:T(8,128)S(1)}, u32[]{:S(2)}) copy-start(f32[128,96]{0,1:T(8,128)S(1)} %psum.14) | copy-start | bytes 147460

commit v2 on v1

v2 whole, which is shorter than its diff:
```python
import functools

import jax
import jax.numpy as jnp
from jax import lax
from jax.experimental import pallas as pl
from jax.experimental.pallas import tpu as pltpu
from jax.sharding import PartitionSpec as P

MESH = pl.DeviceIdType.MESH
VMEM_BYTES = 56 * 2**20
F32, BF16 = jnp.float32, jnp.bfloat16


def ring_place(row, n):
    odd = lax.rem(row, 2)
    up = lax.div(row, 2)
    return (1 - odd) * up + odd * (n - 1 - up)


def ring_row(place, n):
    back = lax.div(place, n // 2)
    return (1 - back) * 2 * place + back * (2 * (n - 1 - place) + 1)


def neighbours(n):
    me = ring_place(lax.axis_index("row"), n)
    after = ring_row(lax.rem(me + 1, n), n)
    before = ring_row(lax.rem(me + n - 1, n), n)
    return me, after, before


def meet(n, m):
    row, col = lax.axis_index("row"), lax.axis_index("col")
    barrier = pltpu.get_barrier_semaphore()
    for d in range(1, n):
        pl.semaphore_signal(
            barrier, inc=1, device_id=(lax.rem(row + d, n), col), device_id_type=MESH
        )
    for d in range(1, m):
        pl.semaphore_signal(
            barrier, inc=1, device_id=(row, lax.rem(col + d, m)), device_id_type=MESH
        )
    pl.semaphore_wait(barrier, n + m - 2)


def split(x):
    high = x.astype(BF16)
    return high, (x - high.astype(F32)).astype(BF16)


def ppmi_parts(counts, row_log, col_total):
    pmi = jnp.log(jnp.maximum(counts.astype(F32), 1.0)) + row_log - jnp.log(col_total)
    ppmi = jnp.where(counts > 0, jnp.maximum(pmi, 0.0), 0.0)
    return jnp.concatenate(split(ppmi), axis=0)


def tile_width(half):
    width = 1024
    while half % width:
        width //= 2
    return width


def columns_of(place, half, width, n):
    return pl.multiple_of(ring_row(place, n) * (2 * width) + half * width, 128)


def counts_copy(counts_ref, held, sem, item, start, width):
    slot = lax.rem(item, 2)
    return pltpu.make_async_copy(
        counts_ref.at[:, pl.ds(start, width)], held.at[slot], sem.at[slot]
    )


def twice(x):
    high, low = split(x)
    return jnp.concatenate(
        [jnp.concatenate([high, high], axis=1), jnp.concatenate([low, low], axis=1)], axis=0
    )


def eliminate(work, k):
    rank, wide = work.shape
    lanes = lax.broadcasted_iota(jnp.int32, (1, wide // 2), 1)
    rows = lax.broadcasted_iota(jnp.int32, (rank, 1), 0)
    now = work[...]
    row = work[pl.ds(k, 1), :]
    column = jnp.sum(jnp.where(lanes == k, now[:, : wide // 2], 0.0), axis=1, keepdims=True)
    pivot = jnp.sum(jnp.where(lanes == k, row[:, : wide // 2], 0.0), axis=1, keepdims=True)
    root = jnp.sqrt(pivot)
    row = row / root
    rest = now - jnp.where(rows > k, column / root, 0.0) * row
    work[...] = jnp.where(rows == k, row, rest)


def round_kernel(
    n, m, counts_ref, row_log_ref, col_ref, sketch_ref, out_ref, upper_ref,
    buf, held, total, images, grams, left, work,
    send_g, recv_g, send_s, recv_s, counts_sem, own_sem,
    send_i, recv_i, send_m, recv_m, ready,
):
    width = buf.shape[3]
    rank = buf.shape[2]
    rows = row_log_ref.shape[0]
    tile = tile_width(width)
    me, after, before = neighbours(n)
    my_row, col = lax.axis_index("row"), lax.axis_index("col")

    def target(way):
        return ((1 - way) * after + way * before, col)

    def gather_item(item):
        extra = lax.max(item - 2, 0)
        far = lax.min(lax.div(item, 2), 1)
        way = far * lax.rem(extra, 2)
        slot = (1 - far) * item + far * (2 + lax.div(extra, 2))
        distance = lax.div(slot, 2)
        odd = lax.rem(slot, 2)
        half = (1 - way) * odd + way * (1 - odd)
        place = lax.rem(me + n + (2 * way - 1) * distance, n)
        return way, slot, columns_of(place, half, width, n)

    def scatter_item(item):
        way = lax.rem(item, 2)
        own = lax.div(item, 2 * n - 2)
        slot = (1 - own) * (n - lax.div(item, 2)) + own * (n + 1)
        distance = (1 - own) * lax.div(slot, 2)
        odd = lax.rem(slot, 2)
        half = (1 - own) * ((1 - way) * odd + way * (1 - odd)) + own * way
        place = lax.rem(me + n + (1 - 2 * way) * distance, n)
        return way, slot, columns_of(place, half, width, n)

    def send_sketch(way, slot):
        return pltpu.make_async_remote_copy(
            src_ref=buf.at[way, slot],
            dst_ref=buf.at[way, slot + 2],
            send_sem=send_g.at[way, slot],
            recv_sem=recv_g.at[way, slot],
            device_id=target(way),
            device_id_type=MESH,
        )

    def send_sums(way, slot):
        return pltpu.make_async_remote_copy(
            src_ref=buf.at[way, slot + 2],
            dst_ref=buf.at[way, slot],
            send_sem=send_s.at[way, slot],
            recv_sem=recv_s.at[way, slot],
            device_id=target(way),
            device_id_type=MESH,
        )

    def gather_counts(item):
        return counts_copy(counts_ref, held, counts_sem, item, gather_item(item)[2], width)

    def scatter_counts(item):
        return counts_copy(counts_ref, held, counts_sem, item, scatter_item(item)[2], width)

    def ppmi_at(item, start, t):
        return ppmi_parts(
            held[lax.rem(item, 2), :, pl.ds(pl.multiple_of(t * tile, tile), tile)],
            row_log_ref[...],
            col_ref[:, pl.ds(pl.multiple_of(start + t * tile, 128), tile)],
        )

    own = [
        pltpu.make_async_copy(
            sketch_ref.at[:, pl.ds((slot if way == 0 else 1 - slot) * width, width)],
            buf.at[way, slot],
            own_sem.at[way, slot],
        )
        for slot in range(2)
        for way in range(2)
    ]
    for copy in own:
        copy.start()
    gather_counts(0).start()
    meet(n, m)
    for at, copy in enumerate(own):
        copy.wait()
        send_sketch(at % 2, at // 2).start()
    total[...] = jnp.zeros_like(total)

    def gather_step(item, carry):
        way, slot, start = gather_item(item)

        @pl.when(item + 1 < 2 * n)
        def _():
            gather_counts(item + 1).start()

        @pl.when(item >= 2)
        def _():
            send_sketch(way, slot - 2).wait_recv()

            @pl.when(slot <= n - 2)
            def _():
                send_sketch(way, slot).start()

        gather_counts(item).wait()

        def piece(t, carry):
            here = pl.ds(pl.multiple_of(t * tile, tile), tile)
            test = jnp.concatenate(split(buf[way, slot, :, here]), axis=0)
            total[...] += lax.dot_general(
                test, ppmi_at(item, start, t), (((1,), (1,)), ((), ())),
                preferred_element_type=F32,
            )
            return carry

        lax.fori_loop(0, width // tile, piece, 0)
        return carry

    lax.fori_loop(0, 2 * n, gather_step, 0)
    scatter_counts(0).start()

    both = total[:rank, :] + total[rank:, :]
    images[col] = both[:, :rows] + both[:, rows:]

    def image_copy(sender, receiver):
        return pltpu.make_async_remote_copy(
            src_ref=images.at[sender],
            dst_ref=images.at[sender],
            send_sem=send_i.at[receiver],
            recv_sem=recv_i.at[sender],
            device_id=(my_row, receiver),
            device_id_type=MESH,
        )

    others = [lax.rem(col + d, m) for d in range(1, m)]
    for other in others:
        image_copy(col, other).start()

    def sketch_sent(slot, carry):
        send_sketch(0, slot).wait_send()
        send_sketch(1, slot).wait_send()
        return carry

    lax.fori_loop(0, n - 1, sketch_sent, 0)
    for way in range(2):
        pl.semaphore_signal(ready, inc=1, device_id=target(way), device_id_type=MESH)
    for other in others:
        image_copy(other, col).wait_recv()
    image = images[0]
    for c in range(1, m):
        image = image + images[c]
    left[...] = twice(image)

    grams[my_row] = lax.dot_general(
        image, image, (((1,), (1,)), ((), ())),
        precision=lax.Precision.HIGHEST, preferred_element_type=F32,
    )

    def gram_copy(sender, receiver):
        return pltpu.make_async_remote_copy(
            src_ref=grams.at[sender],
            dst_ref=grams.at[sender],
            send_sem=send_m.at[receiver],
            recv_sem=recv_m.at[sender],
            device_id=(receiver, col),
            device_id_type=MESH,
        )

    peers = [lax.rem(my_row + d, n) for d in range(1, n)]
    for peer in peers:
        gram_copy(my_row, peer).start()
    pl.semaphore_wait(ready, 2)

    pieces = min(8, n)
    first = n // 2
    wide = work.shape[1] // 2

    def scatter_step(item, carry):
        way, slot, start = scatter_item(item)
        arrives = slot <= n - 2

        @pl.when(item + 1 < 2 * n)
        def _():
            scatter_counts(item + 1).start()

        scatter_counts(item).wait()

        @pl.when(arrives)
        def _():
            send_sums(way, slot).wait_recv()

        def piece(t, carry):
            here = pl.ds(pl.multiple_of(t * tile, tile), tile)
            product = jnp.dot(left[...], ppmi_at(item, start, t), preferred_element_type=F32)
            product = product[:rank] + product[rank:]

            @pl.when(arrives)
            def _():
                buf[way, slot, :, here] = buf[way, slot, :, here] + product

            @pl.when(jnp.logical_not(arrives))
            def _():
                buf[way, slot, :, here] = product

            return carry

        lax.fori_loop(0, width // tile, piece, 0)

        @pl.when(slot <= n)
        def _():
            send_sums(way, slot - 2).start()

        @pl.when(item == first)
        def _():
            for peer in peers:
                gram_copy(peer, my_row).wait_recv()
            gram = grams[0]
            for r in range(1, n):
                gram = gram + grams[r]
            work[...] = jnp.zeros_like(work)
            work[:, :rank] = gram
            shape = (rank, wide)
            same = lax.broadcasted_iota(jnp.int32, shape, 0) == lax.broadcasted_iota(
                jnp.int32, shape, 1
            )
            work[:, wide:] = jnp.where(same, 1.0, 0.0)

        @pl.when(jnp.logical_and(item >= first, item < first + pieces))
        def _():
            steps = rank // pieces

            def turn(k, carry):
                eliminate(work, (item - first) * steps + k)
                return carry

            lax.fori_loop(0, steps, turn, 0)

        return carry

    lax.fori_loop(0, 2 * n, scatter_step, 0)
    above = lax.broadcasted_iota(jnp.int32, (rank, wide), 0) <= lax.broadcasted_iota(
        jnp.int32, (rank, wide), 1
    )
    upper_ref[...] = jnp.where(above, work[:, :wide], 0.0)[:, :rank]
    inverse = twice(work[:, wide:])
    for slot in (1, 0):
        for way in range(2):
            send_sums(way, slot).wait_recv()
    for half in range(2):
        def finish(t, carry, half=half):
            here = pl.ds(pl.multiple_of(t * tile, tile), tile)
            there = pl.ds(pl.multiple_of(half * width + t * tile, tile), tile)
            high, low = split(
                buf[half, n + 1, :, here] + buf[0, half, :, here] + buf[1, 1 - half, :, here]
            )
            gap = jnp.zeros((wide - rank, tile), BF16)
            sums = jnp.concatenate([high, gap, low, gap], axis=0)
            product = jnp.dot(inverse, sums, preferred_element_type=F32)
            out_ref[:, there] = product[:rank] + product[rank:]
            return carry

        lax.fori_loop(0, width // tile, finish, 0)

    def sums_sent(slot, carry):
        send_sums(0, slot).wait_send()
        send_sums(1, slot).wait_send()
        return carry

    lax.fori_loop(0, n - 1, sums_sent, 0)
    for other in others:
        image_copy(col, other).wait_send()
    for peer in peers:
        gram_copy(my_row, peer).wait_send()


def per_device(n, m, counts, row_total, col_total, grand_total, sketch):
    rows, columns = counts.shape
    shard, rank = sketch.shape
    width = shard // 2
    row_log = (jnp.log(grand_total[0]) - jnp.log(row_total))[:, None]
    vmem, anywhere = pl.BlockSpec(memory_space=pltpu.VMEM), pl.BlockSpec(memory_space=pl.ANY)
    dma = pltpu.SemaphoreType.DMA
    padded = (rank + 127) // 128 * 128
    column_factors, upper = pl.pallas_call(
        functools.partial(round_kernel, n, m),
        out_shape=[
            jax.ShapeDtypeStruct((rank, shard), F32),
            jax.ShapeDtypeStruct((rank, rank), F32),
        ],
        in_specs=[anywhere, vmem, vmem, anywhere],
        out_specs=[vmem, vmem],
        scratch_shapes=[
            pltpu.VMEM((2, n + 2, rank, width), F32),
            pltpu.VMEM((2, rows, width), jnp.int32),
            pltpu.VMEM((2 * rank, 2 * rows), F32),
            pltpu.VMEM((m, rank, rows), F32),
            pltpu.VMEM((n, rank, rank), F32),
            pltpu.VMEM((2 * rank, 2 * rows), BF16),
            pltpu.VMEM((rank, 2 * padded), F32),
            dma((2, n - 1)),
            dma((2, n - 1)),
            dma((2, n - 1)),
            dma((2, n - 1)),
            dma((2,)),
            dma((2, 2)),
            dma((m,)),
            dma((m,)),
            dma((n,)),
            dma((n,)),
            pltpu.SemaphoreType.REGULAR,
        ],
        compiler_params=pltpu.CompilerParams(
            collective_id=0, has_side_effects=True, vmem_limit_bytes=VMEM_BYTES
        ),
        cost_estimate=pl.CostEstimate(
            flops=16 * rows * columns * rank,
            bytes_accessed=8 * rows * columns,
            transcendentals=2 * rows * columns,
        ),
        name="power_round",
    )(counts, row_log, col_total[None, :], sketch.T)
    return (column_factors.T, upper.T)


def solution(mesh):
    return jax.shard_map(
        functools.partial(per_device, mesh.shape["row"], mesh.shape["col"]),
        mesh=mesh,
        in_specs=(P("row", "col"), P("row"), P("col"), P(), P(("col", "row"), None)),
        out_specs=(P(("col", "row"), None), P()),
        check_vma=False,
    )
```

time: 562 us -> 510 us (0.907)
  blocking collectives: 47.6 us -> 0 us
  other arithmetic: 18.9 us -> 0.66 us
  Pallas kernels: 485 us -> 501 us
  matrix products: 6.73 us -> 0 us
    psum x2 -> x0, blocking collectives: 47.6 us -> none  [the longest x1 36.9 us: per_device(): gram_matrix = lax.psum(gram_local, 'row')]
    another operation x5 -> x0, other arithmetic: 18.2 us -> none  [the longest x3 9.53 us: per_device(): factor = jnp.linalg.cholesky(gram_matrix)]
    pallas_call x2 -> x1, Pallas kernels: 485 us -> 501 us  [per_device(): pl.pallas_call(functools.partial(round_kernel, n, m), out_shape=[jax.Shap...]
    another operation x1 -> x0, matrix products: 6.5 us -> none  [per_device(): jax.scipy.linalg.solve_triangular(factor, summed, lower=True)]
where the time goes in v2:
time: 510 us; the launch traced here: 509 us
  Pallas kernels  501 us (98%)
  local copies, waits for them, and re-layouts  6.01 us (1%)
    pallas_call x1, Pallas kernels, per_device(): pl.pallas_call(functools.partial(round_kernel, n, m), out_shape=[jax.Shap...  501 us

profile of v2, /device:TPU:0, one launch (start us, length us, event | category | flops | bytes accessed | tf_op | source)
XLA Modules:
  0.0 509.4 jit_solution(8625372285343933025)
XLA Ops:
  1.3 0.7 subtract_bitcast_fusion
  2.0 0.7 copy.7.row_log_ref
  2.7 501.4 %power_round.1 = (f32[96,8192]{1,0:T(8,128)}, f32[96,96]{1,0:T(8,128)}) custom-call(s32[128,65536]{1,0:T(8,128)} %counts_ref.1, f32[128,1]{1,0:T(8,128)} %copy.7.row_log_ref, f32[1,65536]{1,0:T(1,128)} %bitcast.10, f32[96,8192]{1,0:T(8,128)} %bitcast.9), custom_call_target="tpu_custom_call" | custom-call | flops 12884901888 | bytes 67108864 | tf_op jit(solution)/shard_map/power_round/pallas_call | solution.py:379
  504.1 1.5 copy.8
  505.6 3.8 copy.11

commit v3 on v2

--- a/solution.py
+++ b/solution.py
@@ -9,6 +9,8 @@
 
 MESH = pl.DeviceIdType.MESH
 VMEM_BYTES = 56 * 2**20
+PARTS = 4
+AHEAD = 3
 F32, BF16 = jnp.float32, jnp.bfloat16
 
 
@@ -62,12 +64,13 @@
     return width
 
 
-def columns_of(place, half, width, n):
-    return pl.multiple_of(ring_row(place, n) * (2 * width) + half * width, 128)
+def columns_of(place, half, part, width, n):
+    start = ring_row(place, n) * (2 * PARTS * width) + (half * PARTS + part) * width
+    return pl.multiple_of(start, 128)
 
 
 def counts_copy(counts_ref, held, sem, item, start, width):
-    slot = lax.rem(item, 2)
+    slot = lax.rem(item, AHEAD + 1)
     return pltpu.make_async_copy(
         counts_ref.at[:, pl.ds(start, width)], held.at[slot], sem.at[slot]
     )
@@ -106,47 +109,52 @@
     tile = tile_width(width)
     me, after, before = neighbours(n)
     my_row, col = lax.axis_index("row"), lax.axis_index("col")
+    last = (n - 1) * PARTS
+    items = 2 * n * PARTS
 
     def target(way):
         return ((1 - way) * after + way * before, col)
 
     def gather_item(item):
-        extra = lax.max(item - 2, 0)
-        far = lax.min(lax.div(item, 2), 1)
+        extra = lax.max(item - 2 * PARTS, 0)
+        far = lax.min(lax.div(item, 2 * PARTS), 1)
         way = far * lax.rem(extra, 2)
-        slot = (1 - far) * item + far * (2 + lax.div(extra, 2))
+        spot = (1 - far) * item + far * (2 * PARTS + lax.div(extra, 2))
+        slot, part = lax.div(spot, PARTS), lax.rem(spot, PARTS)
         distance = lax.div(slot, 2)
         odd = lax.rem(slot, 2)
         half = (1 - way) * odd + way * (1 - odd)
         place = lax.rem(me + n + (2 * way - 1) * distance, n)
-        return way, slot, columns_of(place, half, width, n)
+        return way, spot, columns_of(place, half, part, width, n)
 
     def scatter_item(item):
         way = lax.rem(item, 2)
-        own = lax.div(item, 2 * n - 2)
-        slot = (1 - own) * (n - lax.div(item, 2)) + own * (n + 1)
+        count = lax.div(item, 2)
+        own = lax.div(count, last)
+        spot = (1 - own) * (last + 2 * PARTS - 1 - count) + own * (2 * PARTS + count)
+        slot, part = lax.div(spot, PARTS), lax.rem(spot, PARTS)
         distance = (1 - own) * lax.div(slot, 2)
         odd = lax.rem(slot, 2)
         half = (1 - own) * ((1 - way) * odd + way * (1 - odd)) + own * way
         place = lax.rem(me + n + (1 - 2 * way) * distance, n)
-        return way, slot, columns_of(place, half, width, n)
-
-    def send_sketch(way, slot):
+        return way, spot, columns_of(place, half, part, width, n)
+
+    def send_sketch(way, spot):
         return pltpu.make_async_remote_copy(
-            src_ref=buf.at[way, slot],
-            dst_ref=buf.at[way, slot + 2],
-            send_sem=send_g.at[way, slot],
-            recv_sem=recv_g.at[way, slot],
+            src_ref=buf.at[way, spot],
+            dst_ref=buf.at[way, spot + 2 * PARTS],
+            send_sem=send_g.at[way, spot],
+            recv_sem=recv_g.at[way, spot],
             device_id=target(way),
             device_id_type=MESH,
         )
 
-    def send_sums(way, slot):
+    def send_sums(way, spot):
         return pltpu.make_async_remote_copy(
-            src_ref=buf.at[way, slot + 2],
-            dst_ref=buf.at[way, slot],
-            send_sem=send_s.at[way, slot],
-            recv_sem=recv_s.at[way, slot],
+            src_ref=buf.at[way, spot + 2 * PARTS],
+            dst_ref=buf.at[way, spot],
+            send_sem=send_s.at[way, spot],
+            recv_sem=recv_s.at[way, spot],
             device_id=target(way),
             device_id_type=MESH,
         )
@@ -159,23 +167,24 @@
 
     def ppmi_at(item, start, t):
         return ppmi_parts(
-            held[lax.rem(item, 2), :, pl.ds(pl.multiple_of(t * tile, tile), tile)],
+            held[lax.rem(item, AHEAD + 1), :, pl.ds(pl.multiple_of(t * tile, tile), tile)],
             row_log_ref[...],
             col_ref[:, pl.ds(pl.multiple_of(start + t * tile, 128), tile)],
         )
 
     own = [
         pltpu.make_async_copy(
-            sketch_ref.at[:, pl.ds((slot if way == 0 else 1 - slot) * width, width)],
-            buf.at[way, slot],
-            own_sem.at[way, slot],
-        )
-        for slot in range(2)
+            sketch_ref.at[:, pl.ds(((spot + way * PARTS) % (2 * PARTS)) * width, width)],
+            buf.at[way, spot],
+            own_sem.at[way, spot],
+        )
+        for spot in range(2 * PARTS)
         for way in range(2)
     ]
     for copy in own:
         copy.start()
-    gather_counts(0).start()
+    for item in range(AHEAD):
+        gather_counts(item).start()
     meet(n, m)
     for at, copy in enumerate(own):
         copy.wait()
@@ -183,25 +192,25 @@
     total[...] = jnp.zeros_like(total)
 
     def gather_step(item, carry):
-        way, slot, start = gather_item(item)
-
-        @pl.when(item + 1 < 2 * n)
-        def _():
-            gather_counts(item + 1).start()
-
-        @pl.when(item >= 2)
-        def _():
-            send_sketch(way, slot - 2).wait_recv()
-
-            @pl.when(slot <= n - 2)
+        way, spot, start = gather_item(item)
+
+        @pl.when(item + AHEAD < items)
+        def _():
+            gather_counts(item + AHEAD).start()
+
+        @pl.when(item >= 2 * PARTS)
+        def _():
+            send_sketch(way, spot - 2 * PARTS).wait_recv()
+
+            @pl.when(spot < last)
             def _():
-                send_sketch(way, slot).start()
+                send_sketch(way, spot).start()
 
         gather_counts(item).wait()
 
         def piece(t, carry):
             here = pl.ds(pl.multiple_of(t * tile, tile), tile)
-            test = jnp.concatenate(split(buf[way, slot, :, here]), axis=0)
+            test = jnp.concatenate(split(buf[way, spot, :, here]), axis=0)
             total[...] += lax.dot_general(
                 test, ppmi_at(item, start, t), (((1,), (1,)), ((), ())),
                 preferred_element_type=F32,
@@ -211,8 +220,9 @@
         lax.fori_loop(0, width // tile, piece, 0)
         return carry
 
-    lax.fori_loop(0, 2 * n, gather_step, 0)
-    scatter_counts(0).start()
+    lax.fori_loop(0, items, gather_step, 0)
+    for item in range(AHEAD):
+        scatter_counts(item).start()
 
     both = total[:rank, :] + total[rank:, :]
     images[col] = both[:, :rows] + both[:, rows:]
@@ -231,12 +241,12 @@
     for other in others:
         image_copy(col, other).start()
 
-    def sketch_sent(slot, carry):
-        send_sketch(0, slot).wait_send()
-        send_sketch(1, slot).wait_send()
-        return carry
-
-    lax.fori_loop(0, n - 1, sketch_sent, 0)
+    def sketch_sent(spot, carry):
+        send_sketch(0, spot).wait_send()
+        send_sketch(1, spot).wait_send()
+        return carry
+
+    lax.fori_loop(0, last, sketch_sent, 0)
     for way in range(2):
         pl.semaphore_signal(ready, inc=1, device_id=target(way), device_id_type=MESH)
     for other in others:
@@ -266,23 +276,23 @@
         gram_copy(my_row, peer).start()
     pl.semaphore_wait(ready, 2)
 
-    pieces = min(8, n)
-    first = n // 2
+    pieces = min(8, n) * PARTS
+    first = n // 2 * PARTS
     wide = work.shape[1] // 2
 
     def scatter_step(item, carry):
-        way, slot, start = scatter_item(item)
-        arrives = slot <= n - 2
-
-        @pl.when(item + 1 < 2 * n)
-        def _():
-            scatter_counts(item + 1).start()
+        way, spot, start = scatter_item(item)
+        arrives = spot < last
+
+        @pl.when(item + AHEAD < items)
+        def _():
+            scatter_counts(item + AHEAD).start()
 
         scatter_counts(item).wait()
 
         @pl.when(arrives)
         def _():
-            send_sums(way, slot).wait_recv()
+            send_sums(way, spot).wait_recv()
 
         def piece(t, carry):
             here = pl.ds(pl.multiple_of(t * tile, tile), tile)
@@ -291,19 +301,19 @@
 
             @pl.when(arrives)
             def _():
-                buf[way, slot, :, here] = buf[way, slot, :, here] + product
+                buf[way, spot, :, here] = buf[way, spot, :, here] + product
 
             @pl.when(jnp.logical_not(arrives))
             def _():
-                buf[way, slot, :, here] = product
+                buf[way, spot, :, here] = product
 
             return carry
 
         lax.fori_loop(0, width // tile, piece, 0)
 
-        @pl.when(slot <= n)
-        def _():
-            send_sums(way, slot - 2).start()
+        @pl.when(spot < last + 2 * PARTS)
+        def _():
+            send_sums(way, spot - 2 * PARTS).start()
 
         @pl.when(item == first)
         def _():
@@ -332,36 +342,51 @@
 
         return carry
 
-    lax.fori_loop(0, 2 * n, scatter_step, 0)
+    lax.fori_loop(0, items, scatter_step, 0)
     above = lax.broadcasted_iota(jnp.int32, (rank, wide), 0) <= lax.broadcasted_iota(
         jnp.int32, (rank, wide), 1
     )
     upper_ref[...] = jnp.where(above, work[:, :wide], 0.0)[:, :rank]
     inverse = twice(work[:, wide:])
-    for slot in (1, 0):
+
+    def arrived(count, carry):
         for way in range(2):
-            send_sums(way, slot).wait_recv()
-    for half in range(2):
-        def finish(t, carry, half=half):
-            here = pl.ds(pl.multiple_of(t * tile, tile), tile)
-            there = pl.ds(pl.multiple_of(half * width + t * tile, tile), tile)
-            high, low = split(
-                buf[half, n + 1, :, here] + buf[0, half, :, here] + buf[1, 1 - half, :, here]
-            )
-            gap = jnp.zeros((wide - rank, tile), BF16)
-            sums = jnp.concatenate([high, gap, low, gap], axis=0)
-            product = jnp.dot(inverse, sums, preferred_element_type=F32)
-            out_ref[:, there] = product[:rank] + product[rank:]
-            return carry
-
-        lax.fori_loop(0, width // tile, finish, 0)
-
-    def sums_sent(slot, carry):
-        send_sums(0, slot).wait_send()
-        send_sums(1, slot).wait_send()
-        return carry
-
-    lax.fori_loop(0, n - 1, sums_sent, 0)
+            send_sums(way, 2 * PARTS - 1 - count).wait_recv()
+        return carry
+
+    def finish(count, carry):
+        part = PARTS - 1 - count
+        for way in range(2):
+            send_sums(way, part).wait_recv()
+        for half in range(2):
+            def piece(t, carry, half=half):
+                here = pl.ds(pl.multiple_of(t * tile, tile), tile)
+                there = (half * PARTS + part) * width + t * tile
+                high, low = split(
+                    buf[half, last + 2 * PARTS + part, :, here]
+                    + buf[0, half * PARTS + part, :, here]
+                    + buf[1, (1 - half) * PARTS + part, :, here]
+                )
+                gap = jnp.zeros((wide - rank, tile), BF16)
+                sums = jnp.concatenate([high, gap, low, gap], axis=0)
+                product = jnp.dot(inverse, sums, preferred_element_type=F32)
+                out_ref[:, pl.ds(pl.multiple_of(there, tile), tile)] = (
+                    product[:rank] + product[rank:]
+                )
+                return carry
+
+            lax.fori_loop(0, width // tile, piece, 0)
+        return carry
+
+    lax.fori_loop(0, PARTS, arrived, 0)
+    lax.fori_loop(0, PARTS, finish, 0)
+
+    def sums_sent(spot, carry):
+        send_sums(0, spot).wait_send()
+        send_sums(1, spot).wait_send()
+        return carry
+
+    lax.fori_loop(0, last, sums_sent, 0)
     for other in others:
         image_copy(col, other).wait_send()
     for peer in peers:
@@ -371,7 +396,7 @@
 def per_device(n, m, counts, row_total, col_total, grand_total, sketch):
     rows, columns = counts.shape
     shard, rank = sketch.shape
-    width = shard // 2
+    width = shard // (2 * PARTS)
     row_log = (jnp.log(grand_total[0]) - jnp.log(row_total))[:, None]
     vmem, anywhere = pl.BlockSpec(memory_space=pltpu.VMEM), pl.BlockSpec(memory_space=pl.ANY)
     dma = pltpu.SemaphoreType.DMA
@@ -385,19 +410,19 @@
         in_specs=[anywhere, vmem, vmem, anywhere],
         out_specs=[vmem, vmem],
         scratch_shapes=[
-            pltpu.VMEM((2, n + 2, rank, width), F32),
-            pltpu.VMEM((2, rows, width), jnp.int32),
+            pltpu.VMEM((2, (n + 2) * PARTS, rank, width), F32),
+            pltpu.VMEM((AHEAD + 1, rows, width), jnp.int32),
             pltpu.VMEM((2 * rank, 2 * rows), F32),
             pltpu.VMEM((m, rank, rows), F32),
             pltpu.VMEM((n, rank, rank), F32),
             pltpu.VMEM((2 * rank, 2 * rows), BF16),
             pltpu.VMEM((rank, 2 * padded), F32),
-            dma((2, n - 1)),
-            dma((2, n - 1)),
-            dma((2, n - 1)),
-            dma((2, n - 1)),
-            dma((2,)),
-            dma((2, 2)),
+            dma((2, (n - 1) * PARTS)),
+            dma((2, (n - 1) * PARTS)),
+            dma((2, (n - 1) * PARTS)),
+            dma((2, (n - 1) * PARTS)),
+            dma((AHEAD + 1,)),
+            dma((2, 2 * PARTS)),
             dma((m,)),
             dma((m,)),
             dma((n,)),

time: 510 us -> 507 us (level)
  no operation moved by 1% of the time
where the time goes in v3:
time: 507 us; the launch traced here: 506 us
  Pallas kernels  498 us (98%)
  local copies, waits for them, and re-layouts  6.01 us (1%)
    pallas_call x1, Pallas kernels, per_device(): pl.pallas_call(functools.partial(round_kernel, n, m), out_shape=[jax.Shap...  498 us

profile of v3, /device:TPU:0, one launch (start us, length us, event | category | flops | bytes accessed | tf_op | source)
XLA Modules:
  0.0 506.4 jit_solution(11349306822218239239)
XLA Ops:
  1.3 0.7 subtract_bitcast_fusion
  2.0 0.7 copy.7.row_log_ref
  2.7 498.4 %power_round.1 = (f32[96,8192]{1,0:T(8,128)}, f32[96,96]{1,0:T(8,128)}) custom-call(s32[128,65536]{1,0:T(8,128)} %counts_ref.1, f32[128,1]{1,0:T(8,128)} %copy.7.row_log_ref, f32[1,65536]{1,0:T(1,128)} %bitcast.10, f32[96,8192]{1,0:T(8,128)} %bitcast.9), custom_call_target="tpu_custom_call" | custom-call | flops 12884901888 | bytes 67108864 | tf_op jit(solution)/shard_map/power_round/pallas_call | solution.py:404
  501.1 1.5 copy.8
  502.6 3.8 copy.11

commit v4 on v3

--- a/solution.py
+++ b/solution.py
@@ -8,7 +8,7 @@
 from jax.sharding import PartitionSpec as P
 
 MESH = pl.DeviceIdType.MESH
-VMEM_BYTES = 56 * 2**20
+VMEM_BYTES = 44 * 2**20
 PARTS = 4
 AHEAD = 3
 F32, BF16 = jnp.float32, jnp.bfloat16
@@ -256,10 +256,7 @@
         image = image + images[c]
     left[...] = twice(image)
 
-    grams[my_row] = lax.dot_general(
-        image, image, (((1,), (1,)), ((), ())),
-        precision=lax.Precision.HIGHEST, preferred_element_type=F32,
-    )
+    total[:rank, :rows] = image
 
     def gram_copy(sender, receiver):
         return pltpu.make_async_remote_copy(
@@ -272,8 +269,6 @@
         )
 
     peers = [lax.rem(my_row + d, n) for d in range(1, n)]
-    for peer in peers:
-        gram_copy(my_row, peer).start()
     pl.semaphore_wait(ready, 2)
 
     pieces = min(8, n) * PARTS
@@ -314,6 +309,16 @@
         @pl.when(spot < last + 2 * PARTS)
         def _():
             send_sums(way, spot - 2 * PARTS).start()
+
+        @pl.when(item == PARTS)
+        def _():
+            mine = total[:rank, :rows]
+            grams[my_row] = lax.dot_general(
+                mine, mine, (((1,), (1,)), ((), ())),
+                precision=lax.Precision.HIGHEST, preferred_element_type=F32,
+            )
+            for peer in peers:
+                gram_copy(my_row, peer).start()
 
         @pl.when(item == first)
         def _():

time: 507 us -> 505 us (level)
  no operation moved by 1% of the time
where the time goes in v4:
time: 505 us; the launch traced here: 504 us
  Pallas kernels  497 us (98%)
  local copies, waits for them, and re-layouts  5.33 us (1%)
    pallas_call x1, Pallas kernels, per_device(): pl.pallas_call(functools.partial(round_kernel, n, m), out_shape=[jax.Shap...  497 us

profile of v4, /device:TPU:0, one launch (start us, length us, event | category | flops | bytes accessed | tf_op | source)
XLA Modules:
  0.0 504.4 jit_solution(4377663941677443730)
XLA Ops:
  1.3 0.7 subtract_bitcast_fusion
  2.0 0.1 copy.7.row_log_ref
  2.1 0.0 copy-start
  2.1 1.9 copy-done
  4.0 0.0 copy-start.1
  4.0 0.9 copy-done.1
  4.9 497.1 %power_round.1 = (f32[96,8192]{1,0:T(8,128)S(1)}, f32[96,96]{1,0:T(8,128)S(1)}) custom-call(s32[128,65536]{1,0:T(8,128)} %counts_ref.1, f32[128,1]{1,0:T(8,128)S(1)} %copy.7.row_log_ref, f32[1,65536]{1,0:T(1,128)S(1)} %bitcast.10, f32[96,8192]{1,0:T(8,128)S(1)} %bitcast.9), custom_call_target="tpu_custom_call" | custom-call | flops 12884901888 | bytes 67108864 | tf_op jit(solution)/shard_map/power_round/pallas_call | solution.py:409
  502.0 0.7 copy.8
  502.7 1.7 copy.11
Async XLA Ops:
  2.1 1.9 copy-start
  4.0 0.9 copy-start.1
